TPU v7x, 128 devices: a whole 4x4x4 slice. The times are simulated.
128 devices in a mesh: section: 2 (over core), expert: 16 (over z, y), head: 4 (over x).
Axes of the slice: x: 4, y: 4, z: 4, core: 2. Of those that a mesh axis runs over, the one named last changes fastest.
Arguments:
- inputs: bfloat16 [2, 2048, 768], P(None, 'expert'), may hold values from -6 to 6
- cotangent: bfloat16 [2, 2048, 768], P(None, 'expert'), may hold values from -6 to 6
- routes: int32 [2, 2, 2048, 2], P('section', None, 'expert'), may hold values from 0 to 31, all different within a row; in each aligned block of 128 rows (0 to 127, 128 to 255, ..., all dimensions but the last counted through in order) at most 12 rows name the same one
- attend_gain: bfloat16 [2, 768], P('section'), may hold values from 0.099609375 to 1.8984375
- query_key_value: bfloat16 [2, 3, 768, 768], P('section', None, None, 'head'), may hold values from -0.21875 to 0.21875
- attend_out: bfloat16 [2, 768, 768], P('section', 'head'), may hold values from -1.75 to 1.75
- position_bias: bfloat16 [2, 12, 32], P('section', 'head'), may hold values from -4 to 4
- mixture_gain: bfloat16 [2, 768], P('section'), may hold values from 0.099609375 to 1.8984375
- router: bfloat16 [2, 768, 32], P('section'), may hold values from -0.15625 to 0.15625
- expert_up: bfloat16 [2, 32, 768, 3072], P('section', 'expert', None, 'head'), may hold values from -0.21875 to 0.21875
- expert_down: bfloat16 [2, 32, 3072, 768], P('section', 'expert', 'head'), may hold values from -0.109375 to 0.109375
Outputs:
- section_output: bfloat16 [2, 2, 2048, 768], P('section', None, 'expert')
- input_grad: float32 [2, 2, 2048, 768], P('section', None, 'expert')
- grad_attend_gain: float32 [2, 768], P('section')
- grad_query_key_value: float32 [2, 3, 768, 768], P('section', None, None, 'head')
- grad_attend_out: float32 [2, 768, 768], P('section', 'head')
- grad_position_bias: float32 [2, 12, 32], P('section', 'head')
- grad_mixture_gain: float32 [2, 768], P('section')
- grad_router: float32 [2, 768, 32], P('section')
- grad_expert_up: float32 [2, 32, 768, 3072], P('section', 'expert', None, 'head')
- grad_expert_down: float32 [2, 32, 3072, 768], P('section', 'expert', 'head')
Inputs may be any that keep to these rules, and one draw needn't show every extreme that they name: `routes`: each token names two different experts. Among the 128 tokens of one sequence (one section, micro-batch and index of expert), no expert is named more than 12 times over both slots, and in every draw some expert is named exactly 12 times by some sequence.
All inputs are finite; a program needn't handle non-finite values.
Results may differ from a plain program's by a relative error of at most 0.028.
Values may be sent and summed in bfloat16 or wider, within the bound.
No kernel may reach another device: no remote copies, remote signals or barrier semaphores. Data moves between devices by JAX's collectives and lax.ppermute only.
A program may use at most 128 MiB of HBM per device.

v0:
```python
import jax
import jax.numpy as jnp
from jax import lax
from jax.sharding import PartitionSpec as P

HEAD_DIM = 64
EPS = 1e-06
NEG = -1e30


def passed_along(array, axis, by):
    length = lax.axis_size(axis)
    pairs = [(i, i + by) for i in range(length) if 0 <= i + by < length]
    return lax.ppermute(array, axis, pairs)


def norm_scale(values):
    return lax.rsqrt(jnp.mean(values * values, axis=-1, keepdims=True) + EPS)


def norm_back(grad_normed, values, scale, gain):
    unit = values * scale
    grad_gain = jnp.sum(grad_normed * unit, axis=0)
    grad_unit = grad_normed * gain
    grad_values = scale * (grad_unit - unit * jnp.mean(grad_unit * unit, axis=-1, keepdims=True))
    return (grad_values, grad_gain)


def position_tables(length, buckets):
    rows = lax.broadcasted_iota(jnp.int32, (length, length), 0)
    cols = lax.broadcasted_iota(jnp.int32, (length, length), 1)
    offset = rows - cols
    levels = lax.broadcasted_iota(jnp.int32, (buckets, length, length), 0)
    onehot = (jnp.clip(offset, 0, buckets - 1)[None] == levels).astype(jnp.bfloat16)
    return (offset >= 0, onehot)


def slot_targets(route_tile, experts, capacity):
    flat = route_tile.reshape(-1)
    levels = lax.broadcasted_iota(jnp.int32, (flat.shape[0], experts), 1)
    onehot = (flat[:, None] == levels).astype(jnp.int32)
    place = jnp.sum((jnp.cumsum(onehot, axis=0) - 1) * onehot, axis=1)
    return flat * capacity + place


def attend_scores(heads, table, causal, onehot):
    bias = jnp.einsum("bst,hb->hst", onehot, table, preferred_element_type=jnp.float32)
    scores = jnp.einsum("shd,thd->hst", heads[0], heads[1], preferred_element_type=jnp.float32)
    scores = scores * HEAD_DIM ** (-0.5) + bias
    return jnp.where(causal[None], scores, NEG)


def attend_forward(normed, proj_weight, out_weight, table, causal, onehot):
    length = normed.shape[0]
    local_heads = table.shape[0]
    projected = jnp.einsum(
        "sd,kde->kse", normed, proj_weight, preferred_element_type=jnp.float32
    ).astype(jnp.bfloat16)
    heads = projected.reshape(3, length, local_heads, HEAD_DIM)
    scores = attend_scores(heads, table, causal, onehot)
    top = jnp.max(scores, axis=-1, keepdims=True)
    weights = jnp.exp(scores - top)
    total = jnp.sum(weights, axis=-1, keepdims=True)
    probs = (weights / total).astype(jnp.bfloat16)
    mixed = jnp.einsum("hst,thd->shd", probs, heads[2], preferred_element_type=jnp.float32)
    mixed = mixed.reshape(length, local_heads * HEAD_DIM).astype(jnp.bfloat16)
    partial_out = jnp.dot(mixed, out_weight, preferred_element_type=jnp.float32)
    return (partial_out, (projected, mixed, top + jnp.log(total)))


def attend_backward(grad_attn, normed, proj_weight, out_weight, table, causal, onehot, saved_attn):
    projected, mixed, log_total = saved_attn
    length = normed.shape[0]
    local_heads = table.shape[0]
    heads = projected.reshape(3, length, local_heads, HEAD_DIM)
    grad_out_weight = jnp.einsum("se,sd->ed", mixed, grad_attn, preferred_element_type=jnp.float32)
    grad_mixed = jnp.einsum("sd,ed->se", grad_attn, out_weight, preferred_element_type=jnp.float32)
    grad_mixed = grad_mixed.astype(jnp.bfloat16).reshape(length, local_heads, HEAD_DIM)
    probs = jnp.exp(attend_scores(heads, table, causal, onehot) - log_total)
    grad_probs = jnp.einsum(
        "shd,thd->hst", grad_mixed, heads[2], preferred_element_type=jnp.float32
    )
    delta = jnp.sum(probs * grad_probs, axis=-1, keepdims=True)
    grad_scores = (probs * (grad_probs - delta)).astype(jnp.bfloat16)
    grad_table = jnp.einsum("bst,hst->hb", onehot, grad_scores, preferred_element_type=jnp.float32)
    factor = HEAD_DIM ** (-0.5)
    grad_query = (
        jnp.einsum("hst,thd->shd", grad_scores, heads[1], preferred_element_type=jnp.float32)
        * factor
    )
    grad_key = (
        jnp.einsum("hst,shd->thd", grad_scores, heads[0], preferred_element_type=jnp.float32)
        * factor
    )
    grad_value = jnp.einsum(
        "hst,shd->thd", probs.astype(jnp.bfloat16), grad_mixed, preferred_element_type=jnp.float32
    )
    grad_projected = (
        jnp.stack([grad_query, grad_key, grad_value])
        .reshape(3, length, local_heads * HEAD_DIM)
        .astype(jnp.bfloat16)
    )
    grad_proj_weight = jnp.einsum(
        "sd,kse->kde", normed, grad_projected, preferred_element_type=jnp.float32
    )
    grad_normed = jnp.einsum(
        "kse,kde->sd", grad_projected, proj_weight, preferred_element_type=jnp.float32
    )
    return (grad_normed, grad_proj_weight, grad_out_weight, grad_table)


def raise_hidden(arrived, up_weight):
    pre_act = jnp.einsum("erd,edf->erf", arrived, up_weight, preferred_element_type=jnp.float32)
    return (pre_act, jax.nn.gelu(pre_act).astype(jnp.bfloat16))


def gate_forward(logits, route_tile, experts):
    levels = lax.broadcasted_iota(jnp.int32, route_tile.shape + (experts,), 2)
    pick = (route_tile[:, :, None] == levels).astype(jnp.float32)
    chosen = jnp.sum(logits[:, None, :] * pick, axis=-1)
    top = jnp.max(chosen, axis=-1, keepdims=True)
    weights = jnp.exp(chosen - top)
    return (weights / jnp.sum(weights, axis=-1, keepdims=True), pick)


def layer_forward(layer_in, route_tile, params, tables):
    gain_a, proj_weight, out_weight, table, gain_m, router_weight, up_weight, down_weight = params
    causal, onehot = tables
    values = layer_in.astype(jnp.float32)
    length, width = values.shape
    experts = router_weight.shape[1]
    local_experts = up_weight.shape[0]
    capacity = 3 * length // experts
    scale_a = norm_scale(values)
    normed_a = (values * scale_a * gain_a).astype(jnp.bfloat16)
    partial_attn, saved_attn = attend_forward(
        normed_a, proj_weight, out_weight, table, causal, onehot
    )
    attended = lax.psum(partial_attn, "head")
    middle = values + attended
    scale_m = norm_scale(middle)
    normed_m = (middle * scale_m * gain_m).astype(jnp.bfloat16)
    logits = jnp.dot(normed_m, router_weight, preferred_element_type=jnp.float32)
    gates, pick = gate_forward(logits, route_tile, experts)
    target = slot_targets(route_tile, experts, capacity)
    buffer = (
        jnp.zeros((experts * capacity, width), jnp.bfloat16)
        .at[target]
        .set(jnp.repeat(normed_m, 2, axis=0))
    )
    arrived = lax.all_to_all(
        buffer.reshape(experts, 1, capacity, width),
        "expert",
        split_axis=0,
        concat_axis=1,
        tiled=True,
    )
    arrived = arrived.reshape(local_experts, -1, width)
    pre_act, hidden = raise_hidden(arrived, up_weight)
    partial_rows = jnp.einsum(
        "erf,efd->erd", hidden, down_weight, preferred_element_type=jnp.float32
    )
    returned = lax.all_to_all(
        partial_rows.reshape(local_experts, -1, capacity, width).astype(jnp.bfloat16),
        "expert",
        split_axis=1,
        concat_axis=0,
        tiled=True,
    ).astype(jnp.float32)
    slot_part = returned.reshape(experts * capacity, width)[target].reshape(length, 2, width)
    slot_out = lax.psum(slot_part.astype(jnp.bfloat16), "head").astype(jnp.float32)
    layer_out = middle + jnp.sum(gates[:, :, None] * slot_out, axis=1)
    owner_saved = (buffer,)
    saved = (
        values,
        scale_a,
        normed_a,
        saved_attn,
        middle,
        scale_m,
        normed_m,
        gates,
        pick,
        target,
        slot_out,
        owner_saved,
    )
    return (layer_out, saved)


def layer_backward(grad_out, saved, params, tables):
    gain_a, proj_weight, out_weight, table, gain_m, router_weight, up_weight, down_weight = params
    causal, onehot = tables
    (
        values,
        scale_a,
        normed_a,
        saved_attn,
        middle,
        scale_m,
        normed_m,
        gates,
        pick,
        target,
        slot_out,
        owner_saved,
    ) = saved
    length, width = values.shape
    experts = router_weight.shape[1]
    local_experts = up_weight.shape[0]
    capacity = 3 * length // experts
    grad_slots = (gates[:, :, None] * grad_out[:, None, :]).astype(jnp.bfloat16)
    grad_gates = jnp.sum(grad_out[:, None, :] * slot_out, axis=-1)
    grad_buffer = (
        jnp.zeros((experts * capacity, width), jnp.bfloat16)
        .at[target]
        .set(grad_slots.reshape(2 * length, width))
    )
    grad_buffer = grad_buffer.reshape(experts, 1, capacity, width)
    row_buffer = owner_saved[0].reshape(experts, 1, capacity, width)
    grad_arrived, arrived = (
        lax.all_to_all(grad_buffer, "expert", split_axis=0, concat_axis=1, tiled=True),
        lax.all_to_all(row_buffer, "expert", split_axis=0, concat_axis=1, tiled=True),
    )
    arrived = arrived.reshape(local_experts, -1, width)
    pre_act, hidden = raise_hidden(arrived, up_weight)
    grad_arrived = grad_arrived.reshape(local_experts, -1, width)
    grad_hidden = jnp.einsum(
        "erd,efd->erf", grad_arrived, down_weight, preferred_element_type=jnp.float32
    )
    unused, gelu_back = jax.vjp(jax.nn.gelu, pre_act)
    grad_pre = gelu_back(grad_hidden)[0].astype(jnp.bfloat16)
    grad_down = jnp.einsum("erf,erd->efd", hidden, grad_arrived, preferred_element_type=jnp.float32)
    grad_up = jnp.einsum("erd,erf->edf", arrived, grad_pre, preferred_element_type=jnp.float32)
    grad_rows = jnp.einsum("erf,edf->erd", grad_pre, up_weight, preferred_element_type=jnp.float32)
    returned = lax.all_to_all(
        grad_rows.reshape(local_experts, -1, capacity, width).astype(jnp.bfloat16),
        "expert",
        split_axis=1,
        concat_axis=0,
        tiled=True,
    ).astype(jnp.float32)
    grad_slot_rows = returned.reshape(experts * capacity, width)[target].reshape(length, 2, width)
    grad_normed_m = lax.psum(jnp.sum(grad_slot_rows, axis=1).astype(jnp.bfloat16), "head").astype(
        jnp.float32
    )
    grad_chosen = gates * (grad_gates - jnp.sum(gates * grad_gates, axis=-1, keepdims=True))
    grad_logits = jnp.sum(grad_chosen[:, :, None] * pick, axis=1).astype(jnp.bfloat16)
    grad_router = jnp.einsum("sd,se->de", normed_m, grad_logits, preferred_element_type=jnp.float32)
    grad_normed_m = grad_normed_m + jnp.einsum(
        "se,de->sd", grad_logits, router_weight, preferred_element_type=jnp.float32
    )
    grad_middle, grad_gain_m = norm_back(grad_normed_m, middle, scale_m, gain_m)
    grad_middle = grad_middle + grad_out
    grad_normed_a, grad_proj_weight, grad_out_weight, grad_table = attend_backward(
        grad_middle.astype(jnp.bfloat16),
        normed_a,
        proj_weight,
        out_weight,
        table,
        causal,
        onehot,
        saved_attn,
    )
    grad_normed_a = lax.psum(grad_normed_a.astype(jnp.bfloat16), "head").astype(jnp.float32)
    grad_values, grad_gain_a = norm_back(grad_normed_a, values, scale_a, gain_a)
    shared = (grad_gain_a, grad_proj_weight, grad_out_weight, grad_table, grad_gain_m, grad_router)
    return (grad_values + grad_middle, shared, (grad_up, grad_down))


def on_device(
    inputs,
    cotangent,
    routes,
    attend_gain,
    query_key_value,
    attend_out,
    position_bias,
    mixture_gain,
    router,
    expert_up,
    expert_down,
):
    micro = inputs.shape[0]
    length = inputs.shape[1]
    params = (
        attend_gain[0].astype(jnp.float32),
        query_key_value[0],
        attend_out[0],
        position_bias[0],
        mixture_gain[0].astype(jnp.float32),
        router[0],
        expert_up[0],
        expert_down[0],
    )
    tables = position_tables(length, position_bias.shape[2])
    first = lax.axis_index("section") == 0
    received = jnp.zeros((length, inputs.shape[2]), jnp.bfloat16)
    outputs = []
    caches = []
    for tick in range(micro + 1):
        layer_in = jnp.where(first, inputs[min(tick, micro - 1)], received)
        route_tile = jnp.where(first, routes[0, min(tick, micro - 1)], routes[0, max(tick - 1, 0)])
        layer_out, saved = layer_forward(layer_in, route_tile, params, tables)
        layer_low = layer_out.astype(jnp.bfloat16)
        outputs.append(layer_low)
        caches.append(saved)
        if tick < micro:
            received = passed_along(layer_low, "section", 1)
    section_output = jnp.stack(
        [jnp.where(first, outputs[index], outputs[index + 1]) for index in range(micro)]
    )[None]
    grad_received = jnp.zeros_like(received)
    shared_total = None
    owned_total = None
    grad_list = []
    for tick in range(micro + 1):
        late = cotangent[min(tick, micro - 1)].astype(jnp.float32)
        if tick == micro:
            late = jnp.zeros_like(late)
        grad_out = jnp.where(first, grad_received.astype(jnp.float32), late)
        saved = jax.tree.map(
            lambda early, later: jnp.where(first, early, later),
            caches[max(tick - 1, 0)],
            caches[min(tick + 1, micro)],
        )
        grad_in, shared, owned = layer_backward(grad_out, saved, params, tables)
        if shared_total is None:
            shared_total = shared
            owned_total = owned
        else:
            shared_total = jax.tree.map(lambda total, extra: total + extra, shared_total, shared)
            owned_total = jax.tree.map(lambda total, extra: total + extra, owned_total, owned)
        grad_list.append(grad_in)
        if tick < micro:
            grad_received = passed_along(grad_in.astype(jnp.bfloat16), "section", -1)
    gain_a, proj_part, out_part, table_part, gain_m, router_part = shared_total
    shared_total = (
        lax.psum(gain_a.astype(jnp.bfloat16), "expert").astype(jnp.float32),
        lax.psum(proj_part.astype(jnp.bfloat16), "expert").astype(jnp.float32),
        lax.psum(out_part.astype(jnp.bfloat16), "expert").astype(jnp.float32),
        lax.psum(table_part.astype(jnp.bfloat16), "expert").astype(jnp.float32),
        lax.psum(gain_m.astype(jnp.bfloat16), "expert").astype(jnp.float32),
        lax.psum(router_part.astype(jnp.bfloat16), "expert").astype(jnp.float32),
    )
    input_grad = jnp.stack(
        [jnp.where(first, grad_list[index + 1], grad_list[index]) for index in range(micro)]
    )[None]
    grad_gain_a, grad_proj, grad_out_weight, grad_table, grad_gain_m, grad_router = shared_total
    grad_up, grad_down = owned_total
    return (
        section_output,
        input_grad,
        grad_gain_a[None],
        grad_proj[None],
        grad_out_weight[None],
        grad_table[None],
        grad_gain_m[None],
        grad_router[None],
        grad_up[None],
        grad_down[None],
    )


def solution(mesh):
    return jax.shard_map(
        on_device,
        mesh=mesh,
        in_specs=(
            P(None, "expert", None),
            P(None, "expert", None),
            P("section", None, "expert", None),
            P("section", None),
            P("section", None, None, "head"),
            P("section", "head", None),
            P("section", "head", None),
            P("section", None),
            P("section", None, None),
            P("section", "expert", None, "head"),
            P("section", "expert", "head", None),
        ),
        out_specs=(
            P("section", None, "expert", None),
            P("section", None, "expert", None),
            P("section", None),
            P("section", None, None, "head"),
            P("section", "head", None),
            P("section", "head", None),
            P("section", None),
            P("section", None, None),
            P("section", "expert", None, "head"),
            P("section", "expert", "head", None),
        ),
        check_vma=False,
    )
```

profile of v0, /device:TPU:0, one launch (start us, length us, event | category | flops | bytes accessed | tf_op | source)
XLA Modules:
  0.0 950.1 jit_solution(12501314368429168360)
XLA Ops:
  22.1 39.1 %all-reduce.16.cloned.1.call-done = f32[128,768]{1,0:T(8,128)} async-done(((f32[128,768]{1,0:T(8,128)}), f32[128,768]{1,0:T(8,128)}) %all-reduce.16.cloned.1.call-update) | async-done | bytes 393232 | tf_op jit(solution)/shard_map/psum | solution.py:139
  68.0 19.2 %all_to_all.189 = bf16[32,1,12,768]{3,2,1,0:T(8,128)(2,1)S(1)} all-to-all(bf16[32,1,12,768]{3,2,1,0:T(8,128)(2,1)} %bitcast.600), channel_id=1, replica_groups=mesh['section'=2,'expert'=16,'head'=4] {'expert'}, dimensions={0} | all-to-all | bytes 1179648 | tf_op jit(solution)/shard_map/all_to_all | solution.py:151
  88.1 3.7 fusion.44
  94.4 3.6 all-to-all-start.1
  98.2 10.2 %all-to-all-done.1 = bf16[2,16,12,768]{3,0,2,1:T(2,128)(2,1)S(1)} async-done(((bf16[2,16,12,768]{3,0,2,1:T(2,128)(2,1)}), bf16[2,16,12,768]{3,0,2,1:T(2,128)(2,1)S(1)}, u32[]{:S(2)}, u32[]{:S(2)}) %all-to-all-start.1) | async-done | bytes 589856 | tf_op jit(solution)/shard_map/all_to_all | solution.py:163
  114.5 38.0 %all-reduce.18.cloned.1.call-done = bf16[128,2,768]{2,1,0:T(2,128)(2,1)} async-done(((bf16[128,2,768]{2,1,0:T(2,128)(2,1)}), bf16[128,2,768]{2,1,0:T(2,128)(2,1)}) %all-reduce.18.cloned.1.call-update) | async-done | bytes 393232 | tf_op jit(solution)/shard_map/psum | solution.py:171
  164.4 40.4 %all-reduce.20.cloned.1.call-done = f32[128,768]{1,0:T(8,128)} async-done(((f32[128,768]{1,0:T(8,128)}), f32[128,768]{1,0:T(8,128)}) %all-reduce.20.cloned.1.call-update) | async-done | bytes 393232 | tf_op jit(solution)/shard_map/psum | solution.py:139
  214.6 7.0 all-to-all-start.7
  225.1 8.9 all-to-all-done.7
  234.0 4.3 all-to-all-start.2
  244.1 5.9 all-to-all-done.2
  250.1 4.3 all-to-all-start.6
  259.3 3.8 fusion.47
  266.0 6.9 all-to-all-start.3
  284.2 5.0 all-to-all-start.8
  310.8 3.0 fusion.217
  313.8 3.1 fusion.176
  317.0 37.1 %all-reduce.36.cloned.1.call-done = (bf16[128,768]{1,0:T(8,128)(2,1)}, bf16[128,2,768]{2,1,0:T(2,128)(2,1)}) async-done(((bf16[128,768]{1,0:T(8,128)(2,1)}, bf16[128,2,768]{2,1,0:T(2,128)(2,1)}), (bf16[128,768]{1,0:T(8,128)(2,1)}, bf16[128,2,768]{2,1,0:T(2,128)(2,1)})) %all-reduce.36.cloned.1.call-update) | async-done | bytes 589840 | tf_op jit(solution)/shard_map/psum | solution.py:244
  354.1 4.0 fusion.170
  369.2 38.2 %all-reduce.24.cloned.1.call-done = bf16[128,768]{1,0:T(8,128)(2,1)} async-done(((bf16[128,768]{1,0:T(8,128)(2,1)}), bf16[128,768]{1,0:T(8,128)(2,1)}) %all-reduce.24.cloned.1.call-update) | async-done | bytes 196624 | tf_op jit(solution)/shard_map/psum | solution.py:265
  420.9 37.7 %all-reduce.22.cloned.1.call-done = f32[128,768]{1,0:T(8,128)} async-done(((f32[128,768]{1,0:T(8,128)}), f32[128,768]{1,0:T(8,128)}) %all-reduce.22.cloned.1.call-update) | async-done | bytes 393232 | tf_op jit(solution)/shard_map/psum | solution.py:139
  464.9 2.9 scatter_custom_fusion.2
  472.0 7.2 all-to-all-start.13
  486.3 5.2 all-to-all-done.13
  491.6 4.5 all-to-all-start.4
  504.0 6.3 all-to-all-done.4
  510.3 4.3 all-to-all-start.10
  520.0 7.7 all-to-all-done.10
  527.6 4.3 all-to-all-start.9
  538.2 2.9 fusion.50
  544.7 7.4 all-to-all-start.5
  562.6 4.8 all-to-all-start.11
  567.5 3.0 fusion.212
  591.9 3.1 fusion.177
  595.1 37.2 %all-reduce.34.cloned.1.call-done = (bf16[128,768]{1,0:T(8,128)(2,1)}, bf16[128,2,768]{2,1,0:T(2,128)(2,1)}) async-done(((bf16[128,768]{1,0:T(8,128)(2,1)}, bf16[128,2,768]{2,1,0:T(2,128)(2,1)}), (bf16[128,768]{1,0:T(8,128)(2,1)}, bf16[128,2,768]{2,1,0:T(2,128)(2,1)})) %all-reduce.34.cloned.1.call-update) | async-done | bytes 589840 | tf_op jit(solution)/shard_map/psum | solution.py:244
  649.4 39.0 %all-reduce.26.cloned.1.call-done = bf16[128,768]{1,0:T(8,128)(2,1)} async-done(((bf16[128,768]{1,0:T(8,128)(2,1)}), bf16[128,768]{1,0:T(8,128)(2,1)}) %all-reduce.26.cloned.1.call-update) | async-done | bytes 196624 | tf_op jit(solution)/shard_map/psum | solution.py:265
  707.3 7.2 all-to-all-start.12
  717.3 11.9 %all-to-all-done.12 = bf16[32,1,12,768]{3,2,1,0:T(8,128)(2,1)} async-done(((bf16[32,1,12,768]{3,2,1,0:T(8,128)(2,1)}), bf16[32,1,12,768]{3,2,1,0:T(8,128)(2,1)}, u32[]{:S(2)}, u32[]{:S(2)}) %all-to-all-start.12) | async-done | bytes 589856 | tf_op jit(solution)/shard_map/all_to_all | solution.py:222
  731.4 3.1 fusion.74
  736.9 4.2 all-to-all-start.14
  741.2 7.2 add_bitcast_fusion
  748.5 4.2 all-to-all-done.14
  762.5 7.3 add_bitcast_fusion.1
  769.7 30.9 %all-reduce.28.cloned.1.call-done = bf16[128,768]{1,0:T(8,128)(2,1)} async-done(((bf16[128,768]{1,0:T(8,128)(2,1)}), bf16[128,768]{1,0:T(8,128)(2,1)}) %all-reduce.28.cloned.1.call-update) | async-done | bytes 196624 | tf_op jit(solution)/shard_map/psum | solution.py:244
  806.6 3.5 fusion.34
  816.8 31.7 %all-reduce.30.cloned.1.call-done = bf16[128,768]{1,0:T(8,128)(2,1)} async-done(((bf16[128,768]{1,0:T(8,128)(2,1)}), bf16[128,768]{1,0:T(8,128)(2,1)}) %all-reduce.30.cloned.1.call-update) | async-done | bytes 196624 | tf_op jit(solution)/shard_map/psum | solution.py:265
  850.9 75.9 %all-reduce = (bf16[1,3,32]{2,1,0:T(4,128)(2,1)}, bf16[1,768]{1,0:T(2,128)(2,1)}, bf16[1,768]{1,0:T(2,128)(2,1)S(1)}, bf16[1,768,32]{1,2,0:T(8,128)(2,1)}) all-reduce(bf16[1,3,32]{2,1,0:T(4,128)(2,1)} %fusion.153, bf16[1,768]{1,0:T(2,128)(2,1)S(1)} %broadcast_in_dim.93, ...), channel_id=1, replica_groups=mesh['section'=2,'expert'=16,'head'=4] {'expert'}, use_global_device_ids=true, to_apply=%region_78.79 | all-reduce | flops 26208 | bytes 104832 | tf_op jit(solution)/shard_map/psum | solution.py:342
  934.2 6.0 all-reduce.32.cloned.1.call-done
  (777 shorter events, 276.6 us)
Async XLA Ops:
  7.2 80.9 %copy-start = (bf16[1,2,768,768]{3,2,1,0:T(8,128)(2,1)S(1)}, bf16[1,2,768,768]{3,2,1,0:T(8,128)(2,1)}, u32[]{:S(2)}) copy-start(bf16[1,2,768,768]{3,2,1,0:T(8,128)(2,1)} %param.20) | copy-start | bytes 7077892
  7.2 54.1 %all-reduce.16.cloned.1.call-start = ((), (), s32[]{:S(2)}) async-start(), calls=%async_computation.15 | async-start | bytes 786432 | tf_op jit(solution)/shard_map/psum | solution.py:139
  8.6 149.8 %copy-start.203 = (f32[128]{0:T(128)}, f32[128]{0:T(128)S(1)}, u32[]{:S(2)}) copy-start(f32[128]{0:T(128)S(1)} %fusion.245) | copy-start | bytes 1540
  9.3 149.7 %copy-start.103 = (f32[768]{0:T(1024)}, f32[768]{0:T(1024)S(1)}, u32[]{:S(2)}) copy-start(f32[768]{0:T(1024)S(1)} %convert_reduce_fusion.1) | copy-start | bytes 9220
  15.5 45.8 %copy-start.14 = (bf16[2,128,768]{2,1,0:T(8,128)(2,1)S(1)}, bf16[2,128,768]{2,1,0:T(8,128)(2,1)}, u32[]{:S(2)}) copy-start(bf16[2,128,768]{2,1,0:T(8,128)(2,1)} %param.11) | copy-start | bytes 1179652
  17.1 96.1 %copy-start.171 = (s32[128,2]{0,1:T(2,128)}, s32[128,2]{0,1:T(2,128)S(1)}, u32[]{:S(2)}) copy-start(s32[128,2]{0,1:T(2,128)S(1)} %get-tuple-element.130) | copy-start | bytes 3076
  20.6 185.8 %copy-start.119 = (f32[768]{0:T(1024)}, f32[768]{0:T(1024)S(1)}, u32[]{:S(2)}) copy-start(f32[768]{0:T(1024)S(1)} %convert_reduce_fusion) | copy-start | bytes 9220
  62.4 143.5 %copy-start.205 = (f32[128]{0:T(128)}, f32[128]{0:T(128)S(1)}, u32[]{:S(2)}) copy-start(f32[128]{0:T(128)S(1)} %multiply_reduce_fusion.8) | copy-start | bytes 1540
  94.4 14.0 %all-to-all-start.1 = ((bf16[2,16,12,768]{3,0,2,1:T(2,128)(2,1)}), bf16[2,16,12,768]{3,0,2,1:T(2,128)(2,1)S(1)}, u32[]{:S(2)}, u32[]{:S(2)}) async-start(bf16[2,16,12,768]{3,0,2,1:T(2,128)(2,1)} %bitcast.613), calls=%async_computation.1 | async-start | bytes 1179648 | tf_op jit(solution)/shard_map/all_to_all | solution.py:163
  97.9 54.5 %all-reduce.18.cloned.1.call-start = ((), (), s32[]{:S(2)}) async-start(), calls=%async_computation.16 | async-start | bytes 786432 | tf_op jit(solution)/shard_map/psum | solution.py:171
  113.2 91.6 %all-reduce.20.cloned.1.call-start = ((), (), s32[]{:S(2)}) async-start(), calls=%async_computation.17 | async-start | bytes 786432 | tf_op jit(solution)/shard_map/psum | solution.py:139
  114.5 44.6 %copy-start.9 = (bf16[1,3,768,192]{2,3,1,0:T(8,128)(2,1)S(1)}, bf16[1,3,768,192]{2,3,1,0:T(8,128)(2,1)}, u32[]{:S(2)}) copy-start(bf16[1,3,768,192]{2,3,1,0:T(8,128)(2,1)} %param.15) | copy-start | bytes 2654212
  155.7 2.5 collective-permute-start
  158.4 48.0 %copy-start.1 = (bf16[128,768]{1,0:T(8,128)(2,1)}, bf16[128,768]{1,0:T(8,128)(2,1)S(1)}, u32[]{:S(2)}) copy-start(bf16[128,768]{1,0:T(8,128)(2,1)S(1)} %get-tuple-element.96) | copy-start | bytes 589828
  214.6 19.4 %all-to-all-start.7 = ((bf16[32,1,12,768]{3,2,1,0:T(8,128)(2,1)}), bf16[32,1,12,768]{3,2,1,0:T(8,128)(2,1)}, u32[]{:S(2)}, u32[]{:S(2)}) async-start(bf16[32,1,12,768]{3,2,1,0:T(8,128)(2,1)} %bitcast.598), calls=%async_computation.7 | async-start | bytes 1572864 | tf_op jit(solution)/shard_map/all_to_all | solution.py:223
  234.0 16.1 %all-to-all-start.2 = ((bf16[32,1,12,768]{3,2,1,0:T(8,128)(2,1)}), bf16[32,1,12,768]{3,2,1,0:T(8,128)(2,1)}, u32[]{:S(2)}, u32[]{:S(2)}) async-start(bf16[32,1,12,768]{3,2,1,0:T(8,128)(2,1)} %bitcast.596), calls=%async_computation.2 | async-start | bytes 1572864 | tf_op jit(solution)/shard_map/all_to_all | solution.py:151
  250.1 15.9 %all-to-all-start.6 = ((bf16[32,1,12,768]{3,2,1,0:T(8,128)(2,1)}), bf16[32,1,12,768]{3,2,1,0:T(8,128)(2,1)}, u32[]{:S(2)}, u32[]{:S(2)}) async-start(bf16[32,1,12,768]{3,2,1,0:T(8,128)(2,1)} %bitcast.80), calls=%async_computation.6 | async-start | bytes 1572864 | tf_op jit(solution)/shard_map/all_to_all | solution.py:222
  266.0 17.4 %all-to-all-start.3 = ((bf16[2,16,12,768]{3,0,2,1:T(2,128)(2,1)}), bf16[2,16,12,768]{3,0,2,1:T(2,128)(2,1)S(1)}, u32[]{:S(2)}, u32[]{:S(2)}) async-start(bf16[2,16,12,768]{3,0,2,1:T(2,128)(2,1)} %bitcast.611), calls=%async_computation.3 | async-start | bytes 1179648 | tf_op jit(solution)/shard_map/all_to_all | solution.py:163
  284.2 15.4 %all-to-all-start.8 = ((bf16[2,16,12,768]{3,0,2,1:T(2,128)(2,1)}), bf16[2,16,12,768]{3,0,2,1:T(2,128)(2,1)S(1)}, u32[]{:S(2)}, u32[]{:S(2)}) async-start(bf16[2,16,12,768]{3,0,2,1:T(2,128)(2,1)} %bitcast.88), calls=%async_computation.8 | async-start | bytes 1179648 | tf_op jit(solution)/shard_map/all_to_all | solution.py:236
  289.1 64.9 %all-reduce.36.cloned.1.call-start = ((), (), s32[]{:S(2)}) async-start(), calls=%async_computation.25 | async-start | bytes 1179648 | tf_op jit(solution)/shard_map/psum | solution.py:244
  310.3 97.2 %all-reduce.24.cloned.1.call-start = ((), (), s32[]{:S(2)}) async-start(), calls=%async_computation.19 | async-start | bytes 393216 | tf_op jit(solution)/shard_map/psum | solution.py:265
  316.9 42.8 %copy-start.2 = (bf16[128,768]{1,0:T(8,128)(2,1)S(1)}, bf16[128,768]{1,0:T(8,128)(2,1)}, u32[]{:S(2)}) copy-start(bf16[128,768]{1,0:T(8,128)(2,1)} %copy-done.1) | copy-start | bytes 589828
  316.9 42.8 %copy-start.16 = (bf16[2,128,768]{2,1,0:T(8,128)(2,1)S(1)}, bf16[2,128,768]{2,1,0:T(8,128)(2,1)}, u32[]{:S(2)}) copy-start(bf16[2,128,768]{2,1,0:T(8,128)(2,1)} %param.11) | copy-start | bytes 1179652
  316.9 42.8 %copy-start.24 = (f32[128,768]{1,0:T(8,128)S(1)}, f32[128,768]{1,0:T(8,128)}, u32[]{:S(2)}) copy-start(f32[128,768]{1,0:T(8,128)} %all-reduce.16.cloned.1.call-done) | copy-start | bytes 1179652
  316.9 42.8 %copy-start.82 = (bf16[1,768,32]{1,2,0:T(8,128)(2,1)S(1)}, bf16[1,768,32]{1,2,0:T(8,128)(2,1)}, u32[]{:S(2)}) copy-start(bf16[1,768,32]{1,2,0:T(8,128)(2,1)} %param.19) | copy-start | bytes 147460
  316.9 42.8 %copy-start.120 = (f32[768]{0:T(1024)S(1)}, f32[768]{0:T(1024)}, u32[]{:S(2)}) copy-start(f32[768]{0:T(1024)} %copy-done.119) | copy-start | bytes 9220
  316.9 42.8 %copy-start.201 = (f32[128]{0:T(128)S(1)}, f32[128]{0:T(128)}, u32[]{:S(2)}) copy-start(f32[128]{0:T(128)} %get-tuple-element.144) | copy-start | bytes 1540
  365.2 93.4 %all-reduce.22.cloned.1.call-start = ((), (), s32[]{:S(2)}) async-start(), calls=%async_computation.18 | async-start | bytes 786432 | tf_op jit(solution)/shard_map/psum | solution.py:139
  367.3 42.1 %collective-permute-start.1 = (bf16[128,768]{1,0:T(8,128)(2,1)S(1)}, bf16[128,768]{1,0:T(8,128)(2,1)}, u32[]{:S(2)}, u32[]{:S(2)}) collective-permute-start(bf16[128,768]{1,0:T(8,128)(2,1)S(1)} %get-tuple-element.84), channel_id=1, source_target_pairs={{0,64},{1,65},{2,66},{3,67},{4,68},{5,69},{6,70},{7,71},{8,72},{9,... | collective-permute-start | bytes 589832 | tf_op jit(solution)/shard_map/ppermute | solution.py:14
  411.4 48.9 %copy-start.5 = (bf16[128,768]{1,0:T(8,128)(2,1)}, bf16[128,768]{1,0:T(8,128)(2,1)S(1)}, u32[]{:S(2)}) copy-start(bf16[128,768]{1,0:T(8,128)(2,1)S(1)} %get-tuple-element.92) | copy-start | bytes 589828
  472.0 19.5 %all-to-all-start.13 = ((bf16[32,1,12,768]{3,2,1,0:T(8,128)(2,1)}), bf16[32,1,12,768]{3,2,1,0:T(8,128)(2,1)}, u32[]{:S(2)}, u32[]{:S(2)}) async-start(bf16[32,1,12,768]{3,2,1,0:T(8,128)(2,1)} %bitcast.129), calls=%async_computation.13 | async-start | bytes 1572864 | tf_op jit(solution)/shard_map/all_to_all | solution.py:223
  481.3 16.1 %collective-permute-start.2 = (bf16[128,768]{1,0:T(8,128)(2,1)}, bf16[128,768]{1,0:T(8,128)(2,1)}, u32[]{:S(2)}, u32[]{:S(2)}) collective-permute-start(bf16[128,768]{1,0:T(8,128)(2,1)} %get-tuple-element.99), channel_id=1, source_target_pairs={{64,0},{65,1},{66,2},{67,3},{68,4},{69,5},{70,6},{71,7},{72,8},{73... | collective-permute-start | bytes 589832 | tf_op jit(solution)/shard_map/ppermute | solution.py:14
  491.6 18.7 %all-to-all-start.4 = ((bf16[32,1,12,768]{3,2,1,0:T(8,128)(2,1)}), bf16[32,1,12,768]{3,2,1,0:T(8,128)(2,1)}, u32[]{:S(2)}, u32[]{:S(2)}) async-start(bf16[32,1,12,768]{3,2,1,0:T(8,128)(2,1)} %bitcast.595), calls=%async_computation.4 | async-start | bytes 1572864 | tf_op jit(solution)/shard_map/all_to_all | solution.py:151
  510.3 17.3 %all-to-all-start.10 = ((bf16[32,1,12,768]{3,2,1,0:T(8,128)(2,1)}), bf16[32,1,12,768]{3,2,1,0:T(8,128)(2,1)}, u32[]{:S(2)}, u32[]{:S(2)}) async-start(bf16[32,1,12,768]{3,2,1,0:T(8,128)(2,1)} %bitcast.594), calls=%async_computation.10 | async-start | bytes 1572864 | tf_op jit(solution)/shard_map/all_to_all | solution.py:223
  527.6 17.1 %all-to-all-start.9 = ((bf16[32,1,12,768]{3,2,1,0:T(8,128)(2,1)}), bf16[32,1,12,768]{3,2,1,0:T(8,128)(2,1)}, u32[]{:S(2)}, u32[]{:S(2)}) async-start(bf16[32,1,12,768]{3,2,1,0:T(8,128)(2,1)} %bitcast.101), calls=%async_computation.9 | async-start | bytes 1572864 | tf_op jit(solution)/shard_map/all_to_all | solution.py:222
  544.7 17.9 %all-to-all-start.5 = ((bf16[2,16,12,768]{3,0,2,1:T(2,128)(2,1)}), bf16[2,16,12,768]{3,0,2,1:T(2,128)(2,1)}, u32[]{:S(2)}, u32[]{:S(2)}) async-start(bf16[2,16,12,768]{3,0,2,1:T(2,128)(2,1)} %bitcast.68), calls=%async_computation.5 | async-start | bytes 1179648 | tf_op jit(solution)/shard_map/all_to_all | solution.py:163
  562.6 15.4 %all-to-all-start.11 = ((bf16[2,16,12,768]{3,0,2,1:T(2,128)(2,1)}), bf16[2,16,12,768]{3,0,2,1:T(2,128)(2,1)}, u32[]{:S(2)}, u32[]{:S(2)}) async-start(bf16[2,16,12,768]{3,0,2,1:T(2,128)(2,1)} %bitcast.610), calls=%async_computation.11 | async-start | bytes 1179648 | tf_op jit(solution)/shard_map/all_to_all | solution.py:236
  567.4 64.8 %all-reduce.34.cloned.1.call-start = ((), (), s32[]{:S(2)}) async-start(), calls=%async_computation.24 | async-start | bytes 1179648 | tf_op jit(solution)/shard_map/psum | solution.py:244
  589.7 98.6 %all-reduce.26.cloned.1.call-start = ((), (), s32[]{:S(2)}) async-start(), calls=%async_computation.20 | async-start | bytes 393216 | tf_op jit(solution)/shard_map/psum | solution.py:265
  646.1 44.0 %copy-start.3 = (bf16[128,768]{1,0:T(8,128)(2,1)S(1)}, bf16[128,768]{1,0:T(8,128)(2,1)}, u32[]{:S(2)}) copy-start(bf16[128,768]{1,0:T(8,128)(2,1)} %copy-done.1) | copy-start | bytes 589828
  646.2 44.0 %copy-start.31 = (f32[128,768]{1,0:T(8,128)S(1)}, f32[128,768]{1,0:T(8,128)}, u32[]{:S(2)}) copy-start(f32[128,768]{1,0:T(8,128)} %copy-done.29) | copy-start | bytes 1179652
  693.2 3.3 collective-permute-start.3
  707.3 22.0 %all-to-all-start.12 = ((bf16[32,1,12,768]{3,2,1,0:T(8,128)(2,1)}), bf16[32,1,12,768]{3,2,1,0:T(8,128)(2,1)}, u32[]{:S(2)}, u32[]{:S(2)}) async-start(bf16[32,1,12,768]{3,2,1,0:T(8,128)(2,1)} %bitcast.597), calls=%async_computation.12 | async-start | bytes 1572864 | tf_op jit(solution)/shard_map/all_to_all | solution.py:222
  736.9 15.8 %all-to-all-start.14 = ((bf16[2,16,12,768]{3,0,2,1:T(2,128)(2,1)}), bf16[2,16,12,768]{3,0,2,1:T(2,128)(2,1)}, u32[]{:S(2)}, u32[]{:S(2)}) async-start(bf16[2,16,12,768]{3,0,2,1:T(2,128)(2,1)} %bitcast.612), calls=%async_computation.14 | async-start | bytes 1179648 | tf_op jit(solution)/shard_map/all_to_all | solution.py:236
  741.2 59.4 %all-reduce.28.cloned.1.call-start = ((), (), s32[]{:S(2)}) async-start(), calls=%async_computation.21 | async-start | bytes 393216 | tf_op jit(solution)/shard_map/psum | solution.py:244
  762.4 86.1 %all-reduce.30.cloned.1.call-start = ((), (), s32[]{:S(2)}) async-start(), calls=%async_computation.22 | async-start | bytes 393216 | tf_op jit(solution)/shard_map/psum | solution.py:265
  806.5 133.6 %all-reduce.32.cloned.1.call-start = ((), (), s32[]{:S(2)}) async-start(), calls=%async_computation.23 | async-start | bytes 2359296 | tf_op jit(solution)/shard_map/psum | solution.py:340
  811.1 121.0 %copy-start.65 = (f32[128,768]{1,0:T(8,128)S(1)}, f32[128,768]{1,0:T(8,128)}, u32[]{:S(2)}) copy-start(f32[128,768]{1,0:T(8,128)} %copy-done.64) | copy-start | bytes 1179652
  (204 other events, 1802.2 us)
Sparse Core Ops, SparseCore 0:
  16.6 44.6 all-reduce.15
  113.3 39.0 all-reduce.17
  162.0 42.7 all-reduce.19
  310.4 43.6 all-reduce.35
  365.3 42.0 all-reduce.23
  415.9 42.6 all-reduce.21
  589.8 42.4 all-reduce.33
  646.2 42.0 all-reduce.25
  762.5 38.0 all-reduce.27
  806.6 41.8 all-reduce.29
  852.5 87.6 all-reduce.31
where the time goes:
time: 963 us; the launch traced here: 950 us
  waiting for transfers between devices  445 us (46%)
  local copies, waits for them, and re-layouts  132 us (14%)
  matrix products  95.4 us (10%)
  blocking collectives  95.1 us (10%)
  other arithmetic  83 us (9%)
  starting transfers between devices  82.3 us (9%)
  between operations  17 us (2%)
    psum x3, waiting for transfers between devices, layer_forward(): attended = lax.psum(partial_attn, 'head')  117 us
    psum x3, waiting for transfers between devices, layer_backward(): lax.psum(grad_normed_a.astype(jnp.bfloat16), 'head').astype(jnp.float32)  109 us
    psum x3, waiting for transfers between devices, layer_backward(): lax.psum(jnp.sum(grad_slot_rows, axis=1).astype(jnp.bfloat16), 'head')  105 us
    psum x1, blocking collectives, on_device(): lax.psum(table_part.astype(jnp.bfloat16), 'expert').astype(jnp.float32)  75.9 us
    psum x1, waiting for transfers between devices, layer_forward(): lax.psum(slot_part.astype(jnp.bfloat16), 'head').astype(jnp.float32)  38 us
    all_to_all x3, waiting for transfers between devices, layer_backward(): lax.all_to_all(row_buffer, 'expert', split_axis=0, concat_axis=1, tiled=T...  21.8 us
  transfers between devices with their start and end apart: 29, of which 26 were waited for; matrix products, arithmetic and copies ran while one was open for 16% of the time, Pallas kernels for 0%

commit v1 on v0

--- a/solution.py
+++ b/solution.py
@@ -148,12 +148,12 @@
         .at[target]
         .set(jnp.repeat(normed_m, 2, axis=0))
     )
-    arrived = lax.all_to_all(
-        buffer.reshape(experts, 1, capacity, width),
-        "expert",
-        split_axis=0,
-        concat_axis=1,
-        tiled=True,
+    xin = buffer.reshape(experts, 1, capacity, width)
+    arrived = jnp.concatenate(
+        jax.lax.all_to_all(
+            jnp.stack(jnp.split(xin, jax.lax.axis_size("expert"), axis=0), axis=0), "expert", 0, 0
+        ),
+        axis=1,
     )
     arrived = arrived.reshape(local_experts, -1, width)
     pre_act, hidden = raise_hidden(arrived, up_weight)

time: 963 us -> 990 us (1.028)
  local copies, waits for them, and re-layouts: 132 us -> 158 us
    another operation x5 -> x59, local copies, waits for them, and re-layouts: 0.38 us -> 23.2 us  [the longest x54 22.9 us: layer_forward(): jnp.stack(jnp.split(xin, jax.lax.axis_size('expert'), axis=0), axis=0)]
    unnamed x447 -> x536, local copies, waits for them, and re-layouts: 15.7 us -> 28 us
  transfers between devices with their start and end apart: 29 -> 29, of which waited for: 26 -> 27; matrix products, arithmetic and copies ran while one was open for 16% -> 17% of each run, Pallas kernels for 0% -> 0%
where the time goes in v1:
time: 990 us; the launch traced here: 976 us
  waiting for transfers between devices  449 us (45%)
  local copies, waits for them, and re-layouts  158 us (16%)
  matrix products  97 us (10%)
  blocking collectives  93.3 us (9%)
  other arithmetic  81.4 us (8%)
  starting transfers between devices  79.4 us (8%)
  between operations  17.8 us (2%)
    psum x3, waiting for transfers between devices, layer_forward(): attended = lax.psum(partial_attn, 'head')  121 us
    psum x3, waiting for transfers between devices, layer_backward(): lax.psum(grad_normed_a.astype(jnp.bfloat16), 'head').astype(jnp.float32)  111 us
    psum x3, waiting for transfers between devices, layer_backward(): lax.psum(jnp.sum(grad_slot_rows, axis=1).astype(jnp.bfloat16), 'head')  106 us
    psum x1, blocking collectives, on_device(): lax.psum(table_part.astype(jnp.bfloat16), 'expert').astype(jnp.float32)  76 us
    psum x1, waiting for transfers between devices, layer_forward(): lax.psum(slot_part.astype(jnp.bfloat16), 'head').astype(jnp.float32)  37.6 us
    unnamed x536, local copies, waits for them, and re-layouts  28 us
    another operation x54, local copies, waits for them, and re-layouts, layer_forward(): jnp.stack(jnp.split(xin, jax.lax.axis_size('expert'), axis=0), axis=0)  22.9 us
    all_to_all x3, waiting for transfers between devices, layer_backward(): lax.all_to_all(row_buffer, 'expert', split_axis=0, concat_axis=1, tiled=T...  21 us
  transfers between devices with their start and end apart: 29, of which 27 were waited for; matrix products, arithmetic and copies ran while one was open for 17% of the time, Pallas kernels for 0%

profile of v1, /device:TPU:0, one launch (start us, length us, event | category | flops | bytes accessed | tf_op | source)
XLA Modules:
  0.0 976.0 jit_solution(983627649566766016)
XLA Ops:
  22.2 39.2 %all-reduce.16.cloned.1.call-done = f32[128,768]{1,0:T(8,128)} async-done(((f32[128,768]{1,0:T(8,128)}), f32[128,768]{1,0:T(8,128)}) %all-reduce.16.cloned.1.call-update) | async-done | bytes 393232 | tf_op jit(solution)/shard_map/psum | solution.py:139
  85.5 17.3 %all_to_all.159 = bf16[16,2,1,12,768]{4,1,3,2,0:T(2,128)(2,1)S(1)} all-to-all(bf16[16,2,1,12,768]{4,1,3,2,0:T(2,128)(2,1)S(1)} %copy.224), channel_id=1, replica_groups=mesh['section'=2,'expert'=16,'head'=4] {'expert'}, dimensions={0} | all-to-all | bytes 1179648 | tf_op jit(solution)/shard_map/all_to_all | solution.py:153
  102.8 3.8 fusion.44
  109.1 3.6 all-to-all-start.1
  113.4 9.7 all-to-all-done.1
  129.3 37.6 %all-reduce.18.cloned.1.call-done = bf16[128,2,768]{2,1,0:T(2,128)(2,1)} async-done(((bf16[128,2,768]{2,1,0:T(2,128)(2,1)}), bf16[128,2,768]{2,1,0:T(2,128)(2,1)}) %all-reduce.18.cloned.1.call-update) | async-done | bytes 393232 | tf_op jit(solution)/shard_map/psum | solution.py:171
  180.3 39.2 %all-reduce.20.cloned.1.call-done = f32[128,768]{1,0:T(8,128)} async-done(((f32[128,768]{1,0:T(8,128)}), f32[128,768]{1,0:T(8,128)}) %all-reduce.20.cloned.1.call-update) | async-done | bytes 393232 | tf_op jit(solution)/shard_map/psum | solution.py:139
  229.7 7.2 all-to-all-start.7
  238.9 10.3 %all-to-all-done.7 = bf16[32,1,12,768]{3,2,1,0:T(8,128)(2,1)} async-done(((bf16[32,1,12,768]{3,2,1,0:T(8,128)(2,1)}), bf16[32,1,12,768]{3,2,1,0:T(8,128)(2,1)}, u32[]{:S(2)}, u32[]{:S(2)}) %all-to-all-start.7) | async-done | bytes 589856 | tf_op jit(solution)/shard_map/all_to_all | solution.py:223
  249.2 4.2 all-to-all-start.2
  259.3 4.7 all-to-all-done.2
  264.0 4.3 all-to-all-start.6
  271.0 3.3 fusion.47
  275.7 4.2 all-to-all-done.6
  279.9 3.8 all-to-all-start.3
  295.0 4.9 all-to-all-start.8
  321.5 3.0 fusion.217
  324.6 3.1 fusion.176
  327.7 37.1 %all-reduce.36.cloned.1.call-done = (bf16[128,768]{1,0:T(8,128)(2,1)}, bf16[128,2,768]{2,1,0:T(2,128)(2,1)}) async-done(((bf16[128,768]{1,0:T(8,128)(2,1)}, bf16[128,2,768]{2,1,0:T(2,128)(2,1)}), (bf16[128,768]{1,0:T(8,128)(2,1)}, bf16[128,2,768]{2,1,0:T(2,128)(2,1)})) %all-reduce.36.cloned.1.call-update) | async-done | bytes 589840 | tf_op jit(solution)/shard_map/psum | solution.py:244
  364.8 4.0 fusion.170
  387.7 40.5 %all-reduce.24.cloned.1.call-done = bf16[128,768]{1,0:T(8,128)(2,1)} async-done(((bf16[128,768]{1,0:T(8,128)(2,1)}), bf16[128,768]{1,0:T(8,128)(2,1)}) %all-reduce.24.cloned.1.call-update) | async-done | bytes 196624 | tf_op jit(solution)/shard_map/psum | solution.py:265
  439.2 42.4 %all-reduce.22.cloned.1.call-done = f32[128,768]{1,0:T(8,128)} async-done(((f32[128,768]{1,0:T(8,128)}), f32[128,768]{1,0:T(8,128)}) %all-reduce.22.cloned.1.call-update) | async-done | bytes 393232 | tf_op jit(solution)/shard_map/psum | solution.py:139
  488.0 2.9 scatter_custom_fusion.2
  503.1 7.0 all-to-all-start.13
  517.9 4.5 all-to-all-done.13
  522.4 4.4 all-to-all-start.4
  537.4 6.5 all-to-all-start.10
  549.3 6.2 all-to-all-done.10
  555.5 4.3 all-to-all-start.9
  562.9 3.1 fusion.50
  571.4 5.3 all-to-all-start.5
  587.2 4.7 all-to-all-start.11
  592.2 3.1 fusion.212
  615.9 3.1 fusion.177
  619.1 38.2 %all-reduce.34.cloned.1.call-done = (bf16[128,768]{1,0:T(8,128)(2,1)}, bf16[128,2,768]{2,1,0:T(2,128)(2,1)}) async-done(((bf16[128,768]{1,0:T(8,128)(2,1)}, bf16[128,2,768]{2,1,0:T(2,128)(2,1)}), (bf16[128,768]{1,0:T(8,128)(2,1)}, bf16[128,2,768]{2,1,0:T(2,128)(2,1)})) %all-reduce.34.cloned.1.call-update) | async-done | bytes 589840 | tf_op jit(solution)/shard_map/psum | solution.py:244
  674.4 39.0 %all-reduce.26.cloned.1.call-done = bf16[128,768]{1,0:T(8,128)(2,1)} async-done(((bf16[128,768]{1,0:T(8,128)(2,1)}), bf16[128,768]{1,0:T(8,128)(2,1)}) %all-reduce.26.cloned.1.call-update) | async-done | bytes 196624 | tf_op jit(solution)/shard_map/psum | solution.py:265
  732.3 7.0 all-to-all-start.12
  742.2 12.5 %all-to-all-done.12 = bf16[32,1,12,768]{3,2,1,0:T(8,128)(2,1)} async-done(((bf16[32,1,12,768]{3,2,1,0:T(8,128)(2,1)}), bf16[32,1,12,768]{3,2,1,0:T(8,128)(2,1)}, u32[]{:S(2)}, u32[]{:S(2)}) %all-to-all-start.12) | async-done | bytes 589856 | tf_op jit(solution)/shard_map/all_to_all | solution.py:222
  756.9 3.1 fusion.74
  762.4 4.2 all-to-all-start.14
  766.9 7.2 add_bitcast_fusion
  774.1 4.4 all-to-all-done.14
  788.3 7.3 add_bitcast_fusion.1
  795.5 30.9 %all-reduce.28.cloned.1.call-done = bf16[128,768]{1,0:T(8,128)(2,1)} async-done(((bf16[128,768]{1,0:T(8,128)(2,1)}), bf16[128,768]{1,0:T(8,128)(2,1)}) %all-reduce.28.cloned.1.call-update) | async-done | bytes 196624 | tf_op jit(solution)/shard_map/psum | solution.py:244
  832.4 3.5 fusion.34
  842.6 31.7 %all-reduce.30.cloned.1.call-done = bf16[128,768]{1,0:T(8,128)(2,1)} async-done(((bf16[128,768]{1,0:T(8,128)(2,1)}), bf16[128,768]{1,0:T(8,128)(2,1)}) %all-reduce.30.cloned.1.call-update) | async-done | bytes 196624 | tf_op jit(solution)/shard_map/psum | solution.py:265
  876.7 76.0 %all-reduce = (bf16[1,3,32]{2,1,0:T(4,128)(2,1)}, bf16[1,768]{1,0:T(2,128)(2,1)}, bf16[1,768]{1,0:T(2,128)(2,1)S(1)}, bf16[1,768,32]{1,2,0:T(8,128)(2,1)}) all-reduce(bf16[1,3,32]{2,1,0:T(4,128)(2,1)} %fusion.153, bf16[1,768]{1,0:T(2,128)(2,1)S(1)} %broadcast_in_dim.93, ...), channel_id=1, replica_groups=mesh['section'=2,'expert'=16,'head'=4] {'expert'}, use_global_device_ids=true, to_apply=%region_78.79 | all-reduce | flops 26208 | bytes 104832 | tf_op jit(solution)/shard_map/psum | solution.py:342
  960.0 6.0 all-reduce.32.cloned.1.call-done
  (912 shorter events, 304.9 us)
Async XLA Ops:
  7.2 95.6 %copy-start = (bf16[1,2,768,768]{3,2,1,0:T(8,128)(2,1)S(1)}, bf16[1,2,768,768]{3,2,1,0:T(8,128)(2,1)}, u32[]{:S(2)}) copy-start(bf16[1,2,768,768]{3,2,1,0:T(8,128)(2,1)} %param.20) | copy-start | bytes 7077892
  7.2 54.1 %all-reduce.16.cloned.1.call-start = ((), (), s32[]{:S(2)}) async-start(), calls=%async_computation.15 | async-start | bytes 786432 | tf_op jit(solution)/shard_map/psum | solution.py:139
  9.3 164.2 %copy-start.109 = (f32[768]{0:T(1024)}, f32[768]{0:T(1024)S(1)}, u32[]{:S(2)}) copy-start(f32[768]{0:T(1024)S(1)} %convert_reduce_fusion.1) | copy-start | bytes 9220
  15.5 45.8 %copy-start.14 = (bf16[2,128,768]{2,1,0:T(8,128)(2,1)S(1)}, bf16[2,128,768]{2,1,0:T(8,128)(2,1)}, u32[]{:S(2)}) copy-start(bf16[2,128,768]{2,1,0:T(8,128)(2,1)} %param.11) | copy-start | bytes 1179652
  17.1 110.8 %copy-start.190 = (s32[128,2]{0,1:T(2,128)}, s32[128,2]{0,1:T(2,128)S(1)}, u32[]{:S(2)}) copy-start(s32[128,2]{0,1:T(2,128)S(1)} %get-tuple-element.178) | copy-start | bytes 3076
  20.6 200.5 %copy-start.121 = (f32[768]{0:T(1024)}, f32[768]{0:T(1024)S(1)}, u32[]{:S(2)}) copy-start(f32[768]{0:T(1024)S(1)} %convert_reduce_fusion) | copy-start | bytes 9220
  63.6 49.7 %copy-start.61 = (bf16[128,768]{1,0:T(8,128)(2,1)}, bf16[128,768]{1,0:T(8,128)(2,1)S(1)}, u32[]{:S(2)}) copy-start(bf16[128,768]{1,0:T(8,128)(2,1)S(1)} %multiply_convert_fusion.14) | copy-start | bytes 589828
  109.1 14.0 %all-to-all-start.1 = ((bf16[2,16,12,768]{3,0,2,1:T(2,128)(2,1)}), bf16[2,16,12,768]{3,0,2,1:T(2,128)(2,1)S(1)}, u32[]{:S(2)}, u32[]{:S(2)}) async-start(bf16[2,16,12,768]{3,0,2,1:T(2,128)(2,1)} %bitcast.602), calls=%async_computation.1 | async-start | bytes 1179648 | tf_op jit(solution)/shard_map/all_to_all | solution.py:163
  112.7 54.3 %all-reduce.18.cloned.1.call-start = ((), (), s32[]{:S(2)}) async-start(), calls=%async_computation.16 | async-start | bytes 786432 | tf_op jit(solution)/shard_map/psum | solution.py:171
  127.9 91.6 %all-reduce.20.cloned.1.call-start = ((), (), s32[]{:S(2)}) async-start(), calls=%async_computation.17 | async-start | bytes 786432 | tf_op jit(solution)/shard_map/psum | solution.py:139
  129.3 43.6 %copy-start.222 = (f32[128]{0:T(128)S(1)}, f32[128]{0:T(128)}, u32[]{:S(2)}) copy-start(f32[128]{0:T(128)} %copy-done.221) | copy-start | bytes 1540
  129.3 44.2 %copy-start.9 = (bf16[1,3,768,192]{2,3,1,0:T(8,128)(2,1)S(1)}, bf16[1,3,768,192]{2,3,1,0:T(8,128)(2,1)}, u32[]{:S(2)}) copy-start(bf16[1,3,768,192]{2,3,1,0:T(8,128)(2,1)} %param.15) | copy-start | bytes 2654212
  170.2 2.5 collective-permute-start
  172.8 48.3 %copy-start.1 = (bf16[128,768]{1,0:T(8,128)(2,1)}, bf16[128,768]{1,0:T(8,128)(2,1)S(1)}, u32[]{:S(2)}) copy-start(bf16[128,768]{1,0:T(8,128)(2,1)S(1)} %get-tuple-element.96) | copy-start | bytes 589828
  177.7 42.9 %copy-start.225 = (f32[128]{0:T(128)S(1)}, f32[128]{0:T(128)}, u32[]{:S(2)}) copy-start(f32[128]{0:T(128)} %copy-done.224) | copy-start | bytes 1540
  229.7 19.5 %all-to-all-start.7 = ((bf16[32,1,12,768]{3,2,1,0:T(8,128)(2,1)}), bf16[32,1,12,768]{3,2,1,0:T(8,128)(2,1)}, u32[]{:S(2)}, u32[]{:S(2)}) async-start(bf16[32,1,12,768]{3,2,1,0:T(8,128)(2,1)} %bitcast.586), calls=%async_computation.7 | async-start | bytes 1572864 | tf_op jit(solution)/shard_map/all_to_all | solution.py:223
  249.2 14.8 %all-to-all-start.2 = ((bf16[16,2,1,12,768]{4,1,3,2,0:T(2,128)(2,1)}), bf16[16,2,1,12,768]{4,1,3,2,0:T(2,128)(2,1)}, u32[]{:S(2)}, u32[]{:S(2)}) async-start(bf16[16,2,1,12,768]{4,1,3,2,0:T(2,128)(2,1)} %copy.234), calls=%async_computation.2 | async-start | bytes 1179648 | tf_op jit(solution)/shard_map/all_to_all | solution.py:153
  264.0 15.9 %all-to-all-start.6 = ((bf16[32,1,12,768]{3,2,1,0:T(8,128)(2,1)}), bf16[32,1,12,768]{3,2,1,0:T(8,128)(2,1)}, u32[]{:S(2)}, u32[]{:S(2)}) async-start(bf16[32,1,12,768]{3,2,1,0:T(8,128)(2,1)} %bitcast.74), calls=%async_computation.6 | async-start | bytes 1572864 | tf_op jit(solution)/shard_map/all_to_all | solution.py:222
  279.9 14.3 %all-to-all-start.3 = ((bf16[2,16,12,768]{3,0,2,1:T(2,128)(2,1)}), bf16[2,16,12,768]{3,0,2,1:T(2,128)(2,1)S(1)}, u32[]{:S(2)}, u32[]{:S(2)}) async-start(bf16[2,16,12,768]{3,0,2,1:T(2,128)(2,1)} %bitcast.601), calls=%async_computation.3 | async-start | bytes 1179648 | tf_op jit(solution)/shard_map/all_to_all | solution.py:163
  295.0 15.4 %all-to-all-start.8 = ((bf16[2,16,12,768]{3,0,2,1:T(2,128)(2,1)}), bf16[2,16,12,768]{3,0,2,1:T(2,128)(2,1)S(1)}, u32[]{:S(2)}, u32[]{:S(2)}) async-start(bf16[2,16,12,768]{3,0,2,1:T(2,128)(2,1)} %bitcast.82), calls=%async_computation.8 | async-start | bytes 1179648 | tf_op jit(solution)/shard_map/all_to_all | solution.py:236
  299.9 64.9 %all-reduce.36.cloned.1.call-start = ((), (), s32[]{:S(2)}) async-start(), calls=%async_computation.25 | async-start | bytes 1179648 | tf_op jit(solution)/shard_map/psum | solution.py:244
  321.0 107.2 %all-reduce.24.cloned.1.call-start = ((), (), s32[]{:S(2)}) async-start(), calls=%async_computation.19 | async-start | bytes 393216 | tf_op jit(solution)/shard_map/psum | solution.py:265
  380.7 47.5 %copy-start.17 = (bf16[2,128,768]{2,1,0:T(8,128)(2,1)S(1)}, bf16[2,128,768]{2,1,0:T(8,128)(2,1)}, u32[]{:S(2)}) copy-start(bf16[2,128,768]{2,1,0:T(8,128)(2,1)} %param.11) | copy-start | bytes 1179652
  382.7 47.4 %copy-start.33 = (f32[128,768]{1,0:T(8,128)S(1)}, f32[128,768]{1,0:T(8,128)}, u32[]{:S(2)}) copy-start(f32[128,768]{1,0:T(8,128)} %copy-done.32) | copy-start | bytes 1179652
  382.7 47.4 %collective-permute-start.1 = (bf16[128,768]{1,0:T(8,128)(2,1)}, bf16[128,768]{1,0:T(8,128)(2,1)}, u32[]{:S(2)}, u32[]{:S(2)}) collective-permute-start(bf16[128,768]{1,0:T(8,128)(2,1)} %get-tuple-element.84), channel_id=1, source_target_pairs={{0,64},{1,65},{2,66},{3,67},{4,68},{5,69},{6,70},{7,71},{8,72},{9,... | collective-permute-start | bytes 589832 | tf_op jit(solution)/shard_map/ppermute | solution.py:14
  385.9 95.7 %all-reduce.22.cloned.1.call-start = ((), (), s32[]{:S(2)}) async-start(), calls=%async_computation.18 | async-start | bytes 786432 | tf_op jit(solution)/shard_map/psum | solution.py:139
  432.0 51.4 %copy-start.5 = (bf16[128,768]{1,0:T(8,128)(2,1)}, bf16[128,768]{1,0:T(8,128)(2,1)S(1)}, u32[]{:S(2)}) copy-start(bf16[128,768]{1,0:T(8,128)(2,1)S(1)} %get-tuple-element.92) | copy-start | bytes 589828
  432.7 97.2 %collective-permute-start.2 = (bf16[128,768]{1,0:T(8,128)(2,1)}, bf16[128,768]{1,0:T(8,128)(2,1)}, u32[]{:S(2)}, u32[]{:S(2)}) collective-permute-start(bf16[128,768]{1,0:T(8,128)(2,1)} %get-tuple-element.147), channel_id=1, source_target_pairs={{64,0},{65,1},{66,2},{67,3},{68,4},{69,5},{70,6},{71,7},{72,8},{73... | collective-permute-start | bytes 589832 | tf_op jit(solution)/shard_map/ppermute | solution.py:14
  437.4 45.3 %copy-start.226 = (f32[128]{0:T(128)S(1)}, f32[128]{0:T(128)}, u32[]{:S(2)}) copy-start(f32[128]{0:T(128)} %copy-done.224) | copy-start | bytes 1540
  437.4 45.3 %copy-start.230 = (f32[128]{0:T(128)S(1)}, f32[128]{0:T(128)}, u32[]{:S(2)}) copy-start(f32[128]{0:T(128)} %copy-done.229) | copy-start | bytes 1540
  437.4 45.9 %copy-start.123 = (f32[768]{0:T(1024)S(1)}, f32[768]{0:T(1024)}, u32[]{:S(2)}) copy-start(f32[768]{0:T(1024)} %copy-done.121) | copy-start | bytes 9220
  503.1 19.3 %all-to-all-start.13 = ((bf16[32,1,12,768]{3,2,1,0:T(8,128)(2,1)}), bf16[32,1,12,768]{3,2,1,0:T(8,128)(2,1)S(1)}, u32[]{:S(2)}, u32[]{:S(2)}) async-start(bf16[32,1,12,768]{3,2,1,0:T(8,128)(2,1)} %bitcast.587), calls=%async_computation.13 | async-start | bytes 1572864 | tf_op jit(solution)/shard_map/all_to_all | solution.py:223
  522.4 14.9 %all-to-all-start.4 = ((bf16[16,2,1,12,768]{4,1,3,2,0:T(2,128)(2,1)}), bf16[16,2,1,12,768]{4,1,3,2,0:T(2,128)(2,1)}, u32[]{:S(2)}, u32[]{:S(2)}) async-start(bf16[16,2,1,12,768]{4,1,3,2,0:T(2,128)(2,1)} %copy.242), calls=%async_computation.4 | async-start | bytes 1179648 | tf_op jit(solution)/shard_map/all_to_all | solution.py:153
  537.4 18.1 %all-to-all-start.10 = ((bf16[32,1,12,768]{3,2,1,0:T(8,128)(2,1)}), bf16[32,1,12,768]{3,2,1,0:T(8,128)(2,1)}, u32[]{:S(2)}, u32[]{:S(2)}) async-start(bf16[32,1,12,768]{3,2,1,0:T(8,128)(2,1)} %bitcast.588), calls=%async_computation.10 | async-start | bytes 1572864 | tf_op jit(solution)/shard_map/all_to_all | solution.py:223
  555.5 15.9 %all-to-all-start.9 = ((bf16[32,1,12,768]{3,2,1,0:T(8,128)(2,1)}), bf16[32,1,12,768]{3,2,1,0:T(8,128)(2,1)}, u32[]{:S(2)}, u32[]{:S(2)}) async-start(bf16[32,1,12,768]{3,2,1,0:T(8,128)(2,1)} %bitcast.589), calls=%async_computation.9 | async-start | bytes 1572864 | tf_op jit(solution)/shard_map/all_to_all | solution.py:222
  571.4 15.8 %all-to-all-start.5 = ((bf16[2,16,12,768]{3,0,2,1:T(2,128)(2,1)}), bf16[2,16,12,768]{3,0,2,1:T(2,128)(2,1)}, u32[]{:S(2)}, u32[]{:S(2)}) async-start(bf16[2,16,12,768]{3,0,2,1:T(2,128)(2,1)} %bitcast.62), calls=%async_computation.5 | async-start | bytes 1179648 | tf_op jit(solution)/shard_map/all_to_all | solution.py:163
  587.2 15.2 %all-to-all-start.11 = ((bf16[2,16,12,768]{3,0,2,1:T(2,128)(2,1)}), bf16[2,16,12,768]{3,0,2,1:T(2,128)(2,1)}, u32[]{:S(2)}, u32[]{:S(2)}) async-start(bf16[2,16,12,768]{3,0,2,1:T(2,128)(2,1)} %bitcast.600), calls=%async_computation.11 | async-start | bytes 1179648 | tf_op jit(solution)/shard_map/all_to_all | solution.py:236
  591.9 65.4 %all-reduce.34.cloned.1.call-start = ((), (), s32[]{:S(2)}) async-start(), calls=%async_computation.24 | async-start | bytes 1179648 | tf_op jit(solution)/shard_map/psum | solution.py:244
  614.2 99.2 %all-reduce.26.cloned.1.call-start = ((), (), s32[]{:S(2)}) async-start(), calls=%async_computation.20 | async-start | bytes 393216 | tf_op jit(solution)/shard_map/psum | solution.py:265
  671.2 44.0 %copy-start.3 = (bf16[128,768]{1,0:T(8,128)(2,1)S(1)}, bf16[128,768]{1,0:T(8,128)(2,1)}, u32[]{:S(2)}) copy-start(bf16[128,768]{1,0:T(8,128)(2,1)} %copy-done.1) | copy-start | bytes 589828
  671.2 44.0 %copy-start.34 = (f32[128,768]{1,0:T(8,128)S(1)}, f32[128,768]{1,0:T(8,128)}, u32[]{:S(2)}) copy-start(f32[128,768]{1,0:T(8,128)} %copy-done.32) | copy-start | bytes 1179652
  718.3 3.3 collective-permute-start.3
  732.3 22.4 %all-to-all-start.12 = ((bf16[32,1,12,768]{3,2,1,0:T(8,128)(2,1)}), bf16[32,1,12,768]{3,2,1,0:T(8,128)(2,1)}, u32[]{:S(2)}, u32[]{:S(2)}) async-start(bf16[32,1,12,768]{3,2,1,0:T(8,128)(2,1)} %bitcast.590), calls=%async_computation.12 | async-start | bytes 1572864 | tf_op jit(solution)/shard_map/all_to_all | solution.py:222
  762.4 16.1 %all-to-all-start.14 = ((bf16[2,16,12,768]{3,0,2,1:T(2,128)(2,1)}), bf16[2,16,12,768]{3,0,2,1:T(2,128)(2,1)}, u32[]{:S(2)}, u32[]{:S(2)}) async-start(bf16[2,16,12,768]{3,0,2,1:T(2,128)(2,1)} %bitcast.603), calls=%async_computation.14 | async-start | bytes 1179648 | tf_op jit(solution)/shard_map/all_to_all | solution.py:236
  766.6 59.8 %all-reduce.28.cloned.1.call-start = ((), (), s32[]{:S(2)}) async-start(), calls=%async_computation.21 | async-start | bytes 393216 | tf_op jit(solution)/shard_map/psum | solution.py:244
  788.2 86.1 %all-reduce.30.cloned.1.call-start = ((), (), s32[]{:S(2)}) async-start(), calls=%async_computation.22 | async-start | bytes 393216 | tf_op jit(solution)/shard_map/psum | solution.py:265
  832.3 133.7 %all-reduce.32.cloned.1.call-start = ((), (), s32[]{:S(2)}) async-start(), calls=%async_computation.23 | async-start | bytes 2359296 | tf_op jit(solution)/shard_map/psum | solution.py:340
  836.9 121.0 %copy-start.69 = (f32[128,768]{1,0:T(8,128)S(1)}, f32[128,768]{1,0:T(8,128)}, u32[]{:S(2)}) copy-start(f32[128,768]{1,0:T(8,128)} %copy-done.68) | copy-start | bytes 1179652
  (226 other events, 1936.1 us)
Sparse Core Ops, SparseCore 0:
  16.6 44.6 all-reduce.15
  128.0 38.8 all-reduce.17
  176.7 42.7 all-reduce.19
  321.1 43.5 all-reduce.35
  386.0 42.1 all-reduce.23
  437.5 44.0 all-reduce.21
  614.3 42.9 all-reduce.33
  671.3 42.0 all-reduce.25
  788.3 38.0 all-reduce.27
  832.4 41.8 all-reduce.29
  878.3 87.6 all-reduce.31
